TPU v7x, 32 devices: a whole 2x2x4 slice. The times are simulated.
32 devices in a mesh: groups: 2 (over x), tm: 16 (over z, y, core).
Axes of the slice: x: 2, y: 2, z: 4, core: 2. Of those that a mesh axis runs over, the one named last changes fastest.
Arguments:
- tokens: bfloat16 [2, 4096, 1152], P('groups', 'tm'), parts along dimension 0, may hold values from -6 to 6
- norm_gain: float32 [1152], replicated, may hold values from 0.5 to 8
- w_qkv: bfloat16 [1152, 1728], P('tm'), may hold values from -0.1875 to 0.1875
- w_out: bfloat16 [1152, 576], P('tm'), may hold values from -0.25 to 0.25
- block_mask: int32 [2, 2, 2], P('groups'), parts along dimension 0, may hold values from 0 to 1
- keep_tiles: int32 [2, 256], P('groups', 'tm'), parts along dimension 0, may hold values 0 or 1
- cotangent: bfloat16 [2, 4096, 1152], P('groups', 'tm'), parts along dimension 0, may hold values from -6 to 6
Outputs:
- mixed: bfloat16 [2, 4096, 1152], P('groups', 'tm'), parts along dimension 0
- grad_tokens: bfloat16 [2, 4096, 1152], P('groups', 'tm'), parts along dimension 0
- grad_qkv: float32 [2304, 1728], P(('groups', 'tm')), parts along dimension 0
- grad_out: float32 [2304, 576], P(('groups', 'tm')), parts along dimension 0
There are 2 independent parts, one for each index of `groups`. A program takes and returns all parts, laid end to end along the dimension named above; an argument that names none is the same for every part. Nothing has to cross between parts.
All inputs are finite; a program needn't handle non-finite values. No bound on the sum of `keep_tiles` on one device may be relied on, other than what follows from the above.
Results may differ from a plain program's by a relative error of at most 0.0055.
The roundings to bfloat16 on the way count: a program that leaves them out, or rounds other values in their place, can miss the bound.
Values may be sent and summed in bfloat16 or wider, within the bound.
A program may use at most 128 MiB of HBM per device.

v0:
```python
import jax
import jax.numpy as jnp
from jax import lax
from jax.sharding import PartitionSpec as P

HD = 72
SPLIT = 4
TB = 2
TILE = 16
EPS = 1e-06


def temporal(qkv_cols, dattn_cols, keep_cols, block_mask, frames):
    videos, per_owner, owners, _ = qkv_cols.shape
    band_count = owners // frames
    heads_n = dattn_cols.shape[-1] // HD
    scale = HD ** (-0.5)
    parts = qkv_cols.reshape(videos, per_owner, frames, band_count, 3, heads_n, HD)
    queries = parts[:, :, :, :, 0]
    key_part = parts[:, :, :, :, 1]
    val_part = parts[:, :, :, :, 2]
    d_out = dattn_cols.reshape(videos, per_owner, frames, band_count, heads_n, HD)
    frame_block = jnp.arange(frames) // TB
    blocks = jnp.repeat(jnp.repeat(block_mask, TB, 1), TB, 2) > 0
    same_block = frame_block[:, None] == frame_block[None, :]
    block_allow = blocks | same_block[None]
    kept = jnp.transpose(keep_cols.reshape(videos, per_owner, frames, band_count) > 0, (0, 1, 3, 2))
    diag_one = jnp.arange(frames)[:, None] == jnp.arange(frames)[None, :]
    allow = block_allow[:, None, None, None, :, :] & (kept[:, :, :, None, None, :] | diag_one)
    scores = (
        jnp.einsum("vrfshd,vrgshd->vrshfg", queries, key_part, preferred_element_type=jnp.float32)
        * scale
    )
    scores = jnp.where(allow, scores, -1e30)
    row_top = jnp.max(scores, -1, keepdims=True)
    expo = jnp.exp(scores - row_top)
    probs = expo / jnp.sum(expo, -1, keepdims=True)
    probs_b = probs.astype(jnp.bfloat16)
    attn = jnp.einsum(
        "vrshfg,vrgshd->vrfshd", probs_b, val_part, preferred_element_type=jnp.float32
    ).astype(jnp.bfloat16)
    dprob = jnp.einsum("vrfshd,vrgshd->vrshfg", d_out, val_part, preferred_element_type=jnp.float32)
    dscore = probs * (dprob - jnp.sum(probs * dprob, -1, keepdims=True))
    dscore_b = dscore.astype(jnp.bfloat16)
    grad_query = (
        jnp.einsum("vrshfg,vrgshd->vrfshd", dscore_b, key_part, preferred_element_type=jnp.float32)
        * scale
    ).astype(jnp.bfloat16)
    grad_key = (
        jnp.einsum("vrshfg,vrfshd->vrgshd", dscore_b, queries, preferred_element_type=jnp.float32)
        * scale
    ).astype(jnp.bfloat16)
    grad_value = jnp.einsum(
        "vrshfg,vrfshd->vrgshd", probs_b, d_out, preferred_element_type=jnp.float32
    ).astype(jnp.bfloat16)
    d_qkv = jnp.stack([grad_query, grad_key, grad_value], axis=4).reshape(
        videos, per_owner, owners, -1
    )
    return (attn.reshape(videos, per_owner, owners, -1), d_qkv)


def per_device(tokens, norm_gain, w_qkv, w_out, block_mask, keep_tiles, cotangent):
    owners = lax.axis_size("tm")
    videos, band_len, model_width = tokens.shape
    per_owner = band_len // owners
    frames = owners // SPLIT
    qkv_full, out_full = (
        lax.all_gather(w_qkv, "tm", axis=0, tiled=True),
        lax.all_gather(w_out, "tm", axis=0, tiled=True),
    )
    tok_float = tokens.astype(jnp.float32)
    inv_rms = lax.rsqrt(jnp.mean(tok_float * tok_float, -1, keepdims=True) + EPS)
    normed = tok_float * inv_rms
    hidden = (normed * norm_gain).astype(jnp.bfloat16)
    keep_tok = jnp.repeat(keep_tiles, TILE, axis=1).reshape(videos, per_owner, owners)
    qkv = jnp.dot(hidden, qkv_full, preferred_element_type=jnp.float32).astype(jnp.bfloat16)
    d_attn = jnp.dot(cotangent, out_full, preferred_element_type=jnp.float32).astype(jnp.bfloat16)
    qkv_cols, dattn_cols, keep_cols = (
        lax.all_to_all(
            qkv.reshape(videos, per_owner, owners, -1),
            "tm",
            split_axis=2,
            concat_axis=2,
            tiled=True,
        ),
        lax.all_to_all(
            d_attn.reshape(videos, per_owner, owners, -1),
            "tm",
            split_axis=2,
            concat_axis=2,
            tiled=True,
        ),
        lax.all_to_all(keep_tok, "tm", split_axis=2, concat_axis=2, tiled=True),
    )
    attn_cols, dqkv_cols = temporal(qkv_cols, dattn_cols, keep_cols, block_mask, frames)
    attn_rows, dqkv_rows = (
        lax.all_to_all(attn_cols, "tm", split_axis=2, concat_axis=2, tiled=True),
        lax.all_to_all(dqkv_cols, "tm", split_axis=2, concat_axis=2, tiled=True),
    )
    attn = attn_rows.reshape(videos, band_len, -1)
    d_qkv = dqkv_rows.reshape(videos, band_len, -1)
    part_qkv = jnp.einsum("vtd,vte->de", hidden, d_qkv, preferred_element_type=jnp.float32)
    part_out = jnp.einsum("vtd,vte->de", cotangent, attn, preferred_element_type=jnp.float32)
    d_hidden = lax.optimization_barrier(
        jnp.einsum("vte,de->vtd", d_qkv, qkv_full, preferred_element_type=jnp.float32).astype(
            jnp.bfloat16
        )
    )
    grad_qkv, grad_out = (
        lax.psum_scatter(part_qkv, "tm", scatter_dimension=0, tiled=True),
        lax.psum_scatter(part_out, "tm", scatter_dimension=0, tiled=True),
    )
    mixed = (
        tok_float + jnp.einsum("vte,de->vtd", attn, out_full, preferred_element_type=jnp.float32)
    ).astype(jnp.bfloat16)
    grad = d_hidden.astype(jnp.float32) * norm_gain
    grad_tokens = cotangent.astype(jnp.float32) + inv_rms * (
        grad - normed * jnp.mean(grad * normed, -1, keepdims=True)
    )
    return (mixed, grad_tokens.astype(jnp.bfloat16), grad_qkv, grad_out)


def solution(mesh):
    placed = (
        P("groups", "tm", None),
        P(),
        P("tm", None),
        P("tm", None),
        P("groups", None, None),
        P("groups", "tm"),
        P("groups", "tm", None),
    )
    return jax.shard_map(
        per_device,
        mesh=mesh,
        in_specs=placed,
        out_specs=(
            P("groups", "tm", None),
            P("groups", "tm", None),
            P(("groups", "tm"), None),
            P(("groups", "tm"), None),
        ),
        check_vma=False,
    )
```

profile of v0, /device:TPU:0, one launch (start us, length us, event | category | flops | bytes accessed | tf_op | source)
XLA Modules:
  0.0 400.1 jit_solution(6253478221850050072)
XLA Ops:
  9.9 7.4 %all-to-all-start.1 = ((s32[1,16,16]{1,0,2:T(1,128)}), s32[1,16,16]{1,0,2:T(1,128)S(1)}, u32[]{:S(2)}, u32[]{:S(2)}) async-start(s32[1,16,16]{1,0,2:T(1,128)} %broadcast_in_dim.16), calls=%async_computation.1 | async-start | bytes 16384 | tf_op jit(solution)/shard_map/all_to_all | solution.py:93
  18.6 33.7 %all-gather.5.cloned.1.call-done = bf16[1152,576]{1,0:T(8,128)(2,1)} async-done(((bf16[72,576]{1,0:T(8,128)(2,1)}), bf16[1152,576]{1,0:T(8,128)(2,1)}) %all-gather.5.cloned.1.call-update) | async-done | bytes 1327120 | tf_op jit(solution)/shard_map/all_gather | solution.py:69
  52.2 2.3 convolution_convert_fusion.4
  55.5 3.5 all-to-all-start.3
  59.1 48.6 %all-gather.3.cloned.1.call-done = bf16[1152,1728]{1,0:T(8,128)(2,1)} async-done(((bf16[72,1728]{1,0:T(8,128)(2,1)}), bf16[1152,1728]{1,0:T(8,128)(2,1)}) %all-gather.3.cloned.1.call-update) | async-done | bytes 3981328 | tf_op jit(solution)/shard_map/all_gather | solution.py:68
  107.7 4.0 convolution_convert_fusion.1
  113.6 3.9 all-to-all-start
  120.1 18.1 %all-to-all-done = bf16[1,16,16,1728]{3,1,0,2:T(8,128)(2,1)S(1)} async-done(((bf16[1,16,16,1728]{3,1,0,2:T(8,128)(2,1)}), bf16[1,16,16,1728]{3,1,0,2:T(8,128)(2,1)S(1)}, u32[]{:S(2)}, u32[]{:S(2)}) %all-to-all-start) | async-done | bytes 884768 | tf_op jit(solution)/shard_map/all_to_all | solution.py:79
  138.2 1.7 reshape.294
  141.4 3.1 fusion.35
  148.8 1.7 fusion.13
  151.7 6.1 %all-to-all-start.2 = ((bf16[1,16,16,576]{3,1,0,2:T(8,128)(2,1)}), bf16[1,16,16,576]{3,1,0,2:T(8,128)(2,1)S(1)}, u32[]{:S(2)}, u32[]{:S(2)}) async-start(bf16[1,16,16,576]{3,1,0,2:T(8,128)(2,1)} %reshape.289), calls=%async_computation.2 | async-start | bytes 655360 | tf_op jit(solution)/shard_map/all_to_all | solution.py:97
  157.8 1.8 fusion.15
  159.6 1.5 pad_maximum_fusion
  161.4 1.9 reshape.290
  163.3 5.6 %all-to-all-done.2 = bf16[1,16,16,576]{3,1,0,2:T(8,128)(2,1)S(1)} async-done(((bf16[1,16,16,576]{3,1,0,2:T(8,128)(2,1)}), bf16[1,16,16,576]{3,1,0,2:T(8,128)(2,1)S(1)}, u32[]{:S(2)}, u32[]{:S(2)}) %all-to-all-start.2) | async-done | bytes 294944 | tf_op jit(solution)/shard_map/all_to_all | solution.py:97
  168.9 3.6 all-to-all-start.4
  172.7 2.0 convolution_bitcast_fusion
  174.8 23.5 %all-to-all-done.4 = bf16[1,16,16,1728]{3,1,0,2:T(8,128)(2,1)S(1)} async-done(((bf16[1,16,16,1728]{3,1,0,2:T(8,128)(2,1)}), bf16[1,16,16,1728]{3,1,0,2:T(8,128)(2,1)S(1)}, u32[]{:S(2)}, u32[]{:S(2)}) %all-to-all-start.4) | async-done | bytes 884768 | tf_op jit(solution)/shard_map/all_to_all | solution.py:98
  199.5 4.6 %fusion.31 = f32[1152,1728]{1,0:T(8,128)} fusion(bf16[256,1728]{1,0:T(8,128)(2,1)S(1)} %bitcast.103, bf16[1,256,1152]{2,1,0:T(8,128)(2,1)S(1)} %copy-done, f32[1152]{0:T(1024)S(1)} %copy-done.10, f32[256]{0:T(256)S(1)} %add_rsqrt_fusion), kind=kOutput, calls=%fused_computation.51 | convolution fusion | flops 1020395520 | bytes 9442816 | tf_op jit(solution)/shard_map/vtd,vte->de/dot_general | solution.py:102
  206.0 1.5 fusion.2
  207.5 3.6 fusion.3
  212.7 73.5 %all-reduce.3.cloned.1.call-done = f32[1152,576]{0,1:T(8,128)} async-done(((f32[1152,576]{0,1:T(8,128)}), f32[1152,576]{0,1:T(8,128)}) %all-reduce.3.cloned.1.call-update) | async-done | bytes 2654224
  288.2 105.4 %reduce-scatter.3.cloned.1.call-done = f32[72,1728]{1,0:T(8,128)} async-done(((f32[1152,1728]{1,0:T(8,128)}), f32[72,1728]{1,0:T(8,128)}) %reduce-scatter.3.cloned.1.call-update) | async-done | bytes 497680 | tf_op jit(solution)/shard_map/reduce_scatter | solution.py:110
  (71 shorter events, 22.8 us)
Async XLA Ops:
  7.2 45.1 %all-gather.5.cloned.1.call-start = ((), (), s32[]{:S(2)}) async-start(), calls=%async_computation.7 | async-start | bytes 1566720 | tf_op jit(solution)/shard_map/all_gather | solution.py:69
  7.9 99.8 %all-gather.3.cloned.1.call-start = ((), (), s32[]{:S(2)}) async-start(), calls=%async_computation.6 | async-start | bytes 4386816 | tf_op jit(solution)/shard_map/all_gather | solution.py:68
  9.9 45.6 %all-to-all-start.1 = ((s32[1,16,16]{1,0,2:T(1,128)}), s32[1,16,16]{1,0,2:T(1,128)S(1)}, u32[]{:S(2)}, u32[]{:S(2)}) async-start(s32[1,16,16]{1,0,2:T(1,128)} %broadcast_in_dim.16), calls=%async_computation.1 | async-start | bytes 16384 | tf_op jit(solution)/shard_map/all_to_all | solution.py:93
  54.5 53.2 %copy-start = (bf16[1,256,1152]{2,1,0:T(8,128)(2,1)S(1)}, bf16[1,256,1152]{2,1,0:T(8,128)(2,1)}, u32[]{:S(2)}) copy-start(bf16[1,256,1152]{2,1,0:T(8,128)(2,1)} %param.7) | copy-start | bytes 1769476
  54.5 53.2 %copy-start.10 = (f32[1152]{0:T(1024)S(1)}, f32[1152]{0:T(1024)}, u32[]{:S(2)}) copy-start(f32[1152]{0:T(1024)} %param.8) | copy-start | bytes 13828
  55.5 58.1 %all-to-all-start.3 = ((bf16[1,16,16,576]{3,1,0,2:T(8,128)(2,1)}), bf16[1,16,16,576]{3,1,0,2:T(8,128)(2,1)S(1)}, u32[]{:S(2)}, u32[]{:S(2)}) async-start(bf16[1,16,16,576]{3,1,0,2:T(8,128)(2,1)} %copy.64), calls=%async_computation.3 | async-start | bytes 655360 | tf_op jit(solution)/shard_map/all_to_all | solution.py:86
  113.6 4.0 copy-start.11
  113.6 24.5 %all-to-all-start = ((bf16[1,16,16,1728]{3,1,0,2:T(8,128)(2,1)}), bf16[1,16,16,1728]{3,1,0,2:T(8,128)(2,1)S(1)}, u32[]{:S(2)}, u32[]{:S(2)}) async-start(bf16[1,16,16,1728]{3,1,0,2:T(8,128)(2,1)} %copy.51), calls=%async_computation | async-start | bytes 1835008 | tf_op jit(solution)/shard_map/all_to_all | solution.py:79
  141.4 3.1 copy-start.8
  144.4 2.6 copy-start.9
  144.4 1.1 copy-start.5
  147.0 1.0 copy-start.6
  151.7 17.2 %all-to-all-start.2 = ((bf16[1,16,16,576]{3,1,0,2:T(8,128)(2,1)}), bf16[1,16,16,576]{3,1,0,2:T(8,128)(2,1)S(1)}, u32[]{:S(2)}, u32[]{:S(2)}) async-start(bf16[1,16,16,576]{3,1,0,2:T(8,128)(2,1)} %reshape.289), calls=%async_computation.2 | async-start | bytes 655360 | tf_op jit(solution)/shard_map/all_to_all | solution.py:97
  157.8 1.8 copy-start.7
  163.3 9.4 %copy-start.2 = (bf16[1,256,1152]{2,1,0:T(8,128)(2,1)S(1)}, bf16[1,256,1152]{2,1,0:T(8,128)(2,1)}, u32[]{:S(2)}) copy-start(bf16[1,256,1152]{2,1,0:T(8,128)(2,1)} %param.13) | copy-start | bytes 1769476
  168.9 29.4 %all-to-all-start.4 = ((bf16[1,16,16,1728]{3,1,0,2:T(8,128)(2,1)}), bf16[1,16,16,1728]{3,1,0,2:T(8,128)(2,1)S(1)}, u32[]{:S(2)}, u32[]{:S(2)}) async-start(bf16[1,16,16,1728]{3,1,0,2:T(8,128)(2,1)} %reshape.290), calls=%async_computation.4 | async-start | bytes 1835008 | tf_op jit(solution)/shard_map/all_to_all | solution.py:98
  172.6 113.6 %all-reduce.3.cloned.1.call-start = ((), (), s32[]{:S(2)}) async-start(), calls=%async_computation.9 | async-start | bytes 5308416
  174.8 218.8 %reduce-scatter.3.cloned.1.call-start = ((), (), s32[]{:S(2)}) async-start(), calls=%async_computation.8 | async-start | bytes 8773632 | tf_op jit(solution)/shard_map/reduce_scatter | solution.py:110
  198.6 1.0 copy-start.3
  204.1 0.7 copy-start.12
  204.1 1.9 copy-start.1
  206.0 1.5 copy-start.4
Sparse Core Ops, SparseCore 0:
  10.1 42.0 all-gather.4
  54.5 53.1 all-gather.2
  177.0 109.1 all-reduce.2
  290.6 102.8 reduce-scatter.2
where the time goes:
time: 401 us; the launch traced here: 400 us
  waiting for transfers between devices  310 us (77%)
  matrix products  27.5 us (7%)
  starting transfers between devices  24.8 us (6%)
  local copies, waits for them, and re-layouts  17.5 us (4%)
  between operations  14.7 us (4%)
  other arithmetic  5.81 us (1%)
    reduce_scatter x1, waiting for transfers between devices, per_device(): lax.psum_scatter(part_qkv, 'tm', scatter_dimension=0, tiled=True)  105 us
    unnamed x5, waiting for transfers between devices  74.9 us
    all_gather x1, waiting for transfers between devices, per_device(): lax.all_gather(w_qkv, 'tm', axis=0, tiled=True)  48.6 us
    all_gather x1, waiting for transfers between devices, per_device(): lax.all_gather(w_out, 'tm', axis=0, tiled=True)  33.7 us
    all_to_all x1, waiting for transfers between devices, per_device(): lax.all_to_all(dqkv_cols, 'tm', split_axis=2, concat_axis=2, tiled=True)  23.5 us
    all_to_all x1, waiting for transfers between devices, per_device(): lax.all_to_all(qkv.reshape(videos, per_owner, owners, -1), 'tm', split_ax...  18.1 us
  transfers between devices with their start and end apart: 9, of which 7 were waited for; matrix products, arithmetic and copies ran while one was open for 9% of the time, Pallas kernels for 0%

commit v1 on v0

--- a/solution.py
+++ b/solution.py
@@ -95,7 +95,12 @@
     attn_cols, dqkv_cols = temporal(qkv_cols, dattn_cols, keep_cols, block_mask, frames)
     attn_rows, dqkv_rows = (
         lax.all_to_all(attn_cols, "tm", split_axis=2, concat_axis=2, tiled=True),
-        lax.all_to_all(dqkv_cols, "tm", split_axis=2, concat_axis=2, tiled=True),
+        jnp.concatenate(
+            lax.all_to_all(
+                jnp.stack(jnp.split(dqkv_cols, lax.axis_size("tm"), axis=2)), "tm", 0, 0
+            ),
+            axis=2,
+        ),
     )
     attn = attn_rows.reshape(videos, band_len, -1)
     d_qkv = dqkv_rows.reshape(videos, band_len, -1)

time: 401 us -> 406 us (1.012)
  local copies, waits for them, and re-layouts: 17.5 us -> 28.7 us
  waiting for transfers between devices: 310 us -> 305 us
    unnamed x29 -> x42, local copies, waits for them, and re-layouts: 4.9 us -> 14.3 us
    all_to_all x1, waiting for transfers between devices: 5.62 us -> 0.01 us  [per_device(): lax.all_to_all(attn_cols, 'tm', split_axis=2, concat_axis=2, tiled=True)]
  transfers between devices with their start and end apart: 9 -> 9, of which waited for: 7 -> 6; matrix products, arithmetic and copies ran while one was open for 9% -> 11% of each run, Pallas kernels for 0% -> 0%
where the time goes in v1:
time: 406 us; the launch traced here: 405 us
  waiting for transfers between devices  305 us (75%)
  local copies, waits for them, and re-layouts  28.7 us (7%)
  starting transfers between devices  27.3 us (7%)
  matrix products  24.6 us (6%)
  between operations  14.7 us (4%)
  other arithmetic  5.19 us (1%)
    reduce_scatter x1, waiting for transfers between devices, per_device(): lax.psum_scatter(part_qkv, 'tm', scatter_dimension=0, tiled=True)  105 us
    unnamed x5, waiting for transfers between devices  74.9 us
    all_gather x1, waiting for transfers between devices, per_device(): lax.all_gather(w_qkv, 'tm', axis=0, tiled=True)  48.6 us
    all_gather x1, waiting for transfers between devices, per_device(): lax.all_gather(w_out, 'tm', axis=0, tiled=True)  33.7 us
    all_to_all x1, waiting for transfers between devices, per_device(): lax.all_to_all(jnp.stack(jnp.split(dqkv_cols, lax.axis_size('tm'), axis=2...  23.5 us
    all_to_all x1, waiting for transfers between devices, per_device(): lax.all_to_all(qkv.reshape(videos, per_owner, owners, -1), 'tm', split_ax...  18.7 us
    unnamed x42, local copies, waits for them, and re-layouts  14.3 us
  transfers between devices with their start and end apart: 9, of which 6 were waited for; matrix products, arithmetic and copies ran while one was open for 11% of the time, Pallas kernels for 0%

profile of v1, /device:TPU:0, one launch (start us, length us, event | category | flops | bytes accessed | tf_op | source)
XLA Modules:
  0.0 405.2 jit_solution(10789971251307477563)
XLA Ops:
  9.9 7.4 %all-to-all-start.1 = ((s32[1,16,16]{1,0,2:T(1,128)}), s32[1,16,16]{1,0,2:T(1,128)S(1)}, u32[]{:S(2)}, u32[]{:S(2)}) async-start(s32[1,16,16]{1,0,2:T(1,128)} %broadcast_in_dim.16), calls=%async_computation.1 | async-start | bytes 16384 | tf_op jit(solution)/shard_map/all_to_all | solution.py:93
  18.6 33.7 %all-gather.5.cloned.1.call-done = bf16[1152,576]{1,0:T(8,128)(2,1)} async-done(((bf16[72,576]{1,0:T(8,128)(2,1)}), bf16[1152,576]{1,0:T(8,128)(2,1)}) %all-gather.5.cloned.1.call-update) | async-done | bytes 1327120 | tf_op jit(solution)/shard_map/all_gather | solution.py:69
  52.2 2.3 convolution_convert_fusion.4
  55.5 3.5 all-to-all-start.3
  59.1 48.6 %all-gather.3.cloned.1.call-done = bf16[1152,1728]{1,0:T(8,128)(2,1)} async-done(((bf16[72,1728]{1,0:T(8,128)(2,1)}), bf16[1152,1728]{1,0:T(8,128)(2,1)}) %all-gather.3.cloned.1.call-update) | async-done | bytes 3981328 | tf_op jit(solution)/shard_map/all_gather | solution.py:68
  107.7 4.0 convolution_convert_fusion.1
  112.3 1.3 copy.397
  113.6 3.9 all-to-all-start
  118.1 1.4 reshape.297
  119.5 18.7 %all-to-all-done = bf16[1,16,16,1728]{3,1,0,2:T(8,128)(2,1)S(1)} async-done(((bf16[1,16,16,1728]{3,1,0,2:T(8,128)(2,1)}), bf16[1,16,16,1728]{3,1,0,2:T(8,128)(2,1)S(1)}, u32[]{:S(2)}, u32[]{:S(2)}) %all-to-all-start) | async-done | bytes 884768 | tf_op jit(solution)/shard_map/all_to_all | solution.py:79
  138.2 1.7 reshape.296
  141.2 2.0 fusion.36
  145.1 1.4 multiply_reduce_fusion
  150.4 6.1 %all-to-all-start.2 = ((bf16[1,16,16,576]{3,1,0,2:T(8,128)(2,1)}), bf16[1,16,16,576]{3,1,0,2:T(8,128)(2,1)S(1)}, u32[]{:S(2)}, u32[]{:S(2)}) async-start(bf16[1,16,16,576]{3,1,0,2:T(8,128)(2,1)} %reshape.292), calls=%async_computation.2 | async-start | bytes 655360 | tf_op jit(solution)/shard_map/all_to_all | solution.py:97
  156.5 1.5 pad_maximum_fusion
  159.5 1.9 fusion.35
  171.5 6.1 %all-to-all-start.4 = ((bf16[16,1,16,1,1728]{4,2,3,1,0:T(8,128)(2,1)}), bf16[16,1,16,1,1728]{4,2,3,1,0:T(8,128)(2,1)S(1)}, u32[]{:S(2)}, u32[]{:S(2)}) async-start(bf16[16,1,16,1,1728]{4,2,3,1,0:T(8,128)(2,1)} %bitcast_dynamic-update-slice_fusion), calls=%async_computation.4 | async-start | bytes 1835008 | tf_op jit(solution)/shard_map/all_to_all | solution.py:99
  177.8 2.0 convolution_bitcast_fusion
  179.9 23.5 %all-to-all-done.4 = bf16[16,1,16,1,1728]{4,2,3,1,0:T(8,128)(2,1)S(1)} async-done(((bf16[16,1,16,1,1728]{4,2,3,1,0:T(8,128)(2,1)}), bf16[16,1,16,1,1728]{4,2,3,1,0:T(8,128)(2,1)S(1)}, u32[]{:S(2)}, u32[]{:S(2)}) %all-to-all-start.4) | async-done | bytes 884768 | tf_op jit(solution)/shard_map/all_to_all | solution.py:99
  204.7 4.6 %fusion.31 = f32[1152,1728]{1,0:T(8,128)} fusion(bf16[256,1728]{1,0:T(8,128)(2,1)S(1)} %bitcast.134, bf16[1,256,1152]{2,1,0:T(8,128)(2,1)S(1)} %copy-done, f32[1152]{0:T(1024)S(1)} %copy-done.9, f32[256]{0:T(256)S(1)} %add_rsqrt_fusion), kind=kOutput, calls=%fused_computation.51 | convolution fusion | flops 1020395520 | bytes 9442816 | tf_op jit(solution)/shard_map/vtd,vte->de/dot_general | solution.py:107
  211.2 1.5 fusion.2
  212.6 3.6 fusion.3
  217.8 73.5 %all-reduce.3.cloned.1.call-done = f32[1152,576]{0,1:T(8,128)} async-done(((f32[1152,576]{0,1:T(8,128)}), f32[1152,576]{0,1:T(8,128)}) %all-reduce.3.cloned.1.call-update) | async-done | bytes 2654224
  293.3 105.4 %reduce-scatter.3.cloned.1.call-done = f32[72,1728]{1,0:T(8,128)} async-done(((f32[1152,1728]{1,0:T(8,128)}), f32[72,1728]{1,0:T(8,128)}) %reduce-scatter.3.cloned.1.call-update) | async-done | bytes 497680 | tf_op jit(solution)/shard_map/reduce_scatter | solution.py:115
  (86 shorter events, 30.9 us)
Async XLA Ops:
  7.2 45.1 %all-gather.5.cloned.1.call-start = ((), (), s32[]{:S(2)}) async-start(), calls=%async_computation.7 | async-start | bytes 1566720 | tf_op jit(solution)/shard_map/all_gather | solution.py:69
  7.9 99.8 %all-gather.3.cloned.1.call-start = ((), (), s32[]{:S(2)}) async-start(), calls=%async_computation.6 | async-start | bytes 4386816 | tf_op jit(solution)/shard_map/all_gather | solution.py:68
  9.9 45.6 %all-to-all-start.1 = ((s32[1,16,16]{1,0,2:T(1,128)}), s32[1,16,16]{1,0,2:T(1,128)S(1)}, u32[]{:S(2)}, u32[]{:S(2)}) async-start(s32[1,16,16]{1,0,2:T(1,128)} %broadcast_in_dim.16), calls=%async_computation.1 | async-start | bytes 16384 | tf_op jit(solution)/shard_map/all_to_all | solution.py:93
  54.5 53.2 %copy-start = (bf16[1,256,1152]{2,1,0:T(8,128)(2,1)S(1)}, bf16[1,256,1152]{2,1,0:T(8,128)(2,1)}, u32[]{:S(2)}) copy-start(bf16[1,256,1152]{2,1,0:T(8,128)(2,1)} %param.7) | copy-start | bytes 1769476
  54.5 53.2 %copy-start.9 = (f32[1152]{0:T(1024)S(1)}, f32[1152]{0:T(1024)}, u32[]{:S(2)}) copy-start(f32[1152]{0:T(1024)} %param.8) | copy-start | bytes 13828
  55.5 58.1 %all-to-all-start.3 = ((bf16[1,16,16,576]{3,1,0,2:T(8,128)(2,1)}), bf16[1,16,16,576]{3,1,0,2:T(8,128)(2,1)S(1)}, u32[]{:S(2)}, u32[]{:S(2)}) async-start(bf16[1,16,16,576]{3,1,0,2:T(8,128)(2,1)} %copy.410), calls=%async_computation.3 | async-start | bytes 655360 | tf_op jit(solution)/shard_map/all_to_all | solution.py:86
  113.6 4.0 copy-start.10
  113.6 24.5 %all-to-all-start = ((bf16[1,16,16,1728]{3,1,0,2:T(8,128)(2,1)}), bf16[1,16,16,1728]{3,1,0,2:T(8,128)(2,1)S(1)}, u32[]{:S(2)}, u32[]{:S(2)}) async-start(bf16[1,16,16,1728]{3,1,0,2:T(8,128)(2,1)} %copy.397), calls=%async_computation | async-start | bytes 1835008 | tf_op jit(solution)/shard_map/all_to_all | solution.py:79
  141.2 2.0 copy-start.6
  141.2 2.0 copy-start.5
  143.1 1.0 copy-start.8
  146.5 1.0 copy-start.7
  150.4 21.1 %all-to-all-start.2 = ((bf16[1,16,16,576]{3,1,0,2:T(8,128)(2,1)}), bf16[1,16,16,576]{3,1,0,2:T(8,128)(2,1)S(1)}, u32[]{:S(2)}, u32[]{:S(2)}) async-start(bf16[1,16,16,576]{3,1,0,2:T(8,128)(2,1)} %reshape.292), calls=%async_computation.2 | async-start | bytes 655360 | tf_op jit(solution)/shard_map/all_to_all | solution.py:97
  171.5 6.3 %copy-start.2 = (bf16[1,256,1152]{2,1,0:T(8,128)(2,1)S(1)}, bf16[1,256,1152]{2,1,0:T(8,128)(2,1)}, u32[]{:S(2)}) copy-start(bf16[1,256,1152]{2,1,0:T(8,128)(2,1)} %param.13) | copy-start | bytes 1769476
  171.5 31.9 %all-to-all-start.4 = ((bf16[16,1,16,1,1728]{4,2,3,1,0:T(8,128)(2,1)}), bf16[16,1,16,1,1728]{4,2,3,1,0:T(8,128)(2,1)S(1)}, u32[]{:S(2)}, u32[]{:S(2)}) async-start(bf16[16,1,16,1,1728]{4,2,3,1,0:T(8,128)(2,1)} %bitcast_dynamic-update-slice_fusion), calls=%async_computation.4 | async-start | bytes 1835008 | tf_op jit(solution)/shard_map/all_to_all | solution.py:99
  177.7 113.6 %all-reduce.3.cloned.1.call-start = ((), (), s32[]{:S(2)}) async-start(), calls=%async_computation.9 | async-start | bytes 5308416
  179.9 218.8 %reduce-scatter.3.cloned.1.call-start = ((), (), s32[]{:S(2)}) async-start(), calls=%async_computation.8 | async-start | bytes 8773632 | tf_op jit(solution)/shard_map/reduce_scatter | solution.py:115
  203.7 1.0 copy-start.3
  209.3 0.7 copy-start.11
  209.3 1.9 copy-start.1
  211.2 1.5 copy-start.4
Sparse Core Ops, SparseCore 0:
  10.1 42.0 all-gather.4
  54.5 53.1 all-gather.2
  182.1 109.1 all-reduce.2
  295.8 102.8 reduce-scatter.2
